TPU v7x, 32 devices: a whole 2x2x4 slice. The times are simulated.
32 devices in a mesh: mom: 2 (over x), en: 16 (over z, y, core).
Axes of the slice: x: 2, y: 2, z: 4, core: 2. Of those that a mesh axis runs over, the one named last changes fastest.
Arguments:
- green: bfloat16 [2, 128, 2, 2, 64, 128], P('mom', 'en'), may hold values from -6 to 6
- pair_index: int32 [2, 4], replicated, may hold values from 0 to 1
- pair_weight: float32 [2, 4], replicated, may hold values from 0.1 to 0.4
- phonon_offset: int32 [4], replicated, may hold values from 1 to 4, as said below
- occupation: float32 [4], replicated, may hold values from 0.2 to 3
- vertex: bfloat16 [4, 8, 64, 64], replicated, may hold values from -0.75 to 0.75
- block_atoms: int32 [2, 2], replicated, may hold values from 0 to 7
Outputs:
- self_energy: bfloat16 [2, 128, 2, 2, 64, 128], P('mom', 'en')
Inputs may be any that keep to these rules, and one draw needn't show every extreme that they name: `phonon_offset`: every mode's offset lies in 1 to 4, and some mode's offset is 4.
All inputs are finite; a program needn't handle non-finite values.
Results may differ from a plain program's by a relative error of at most 0.015.
Values may be sent and summed in bfloat16 or wider, within the bound.
A program may use at most 64 MiB of HBM per device.

v0:
```python
import jax
import jax.numpy as jnp
from jax import lax
from jax.sharding import PartitionSpec as P

OFF_MAX = 4


def from_behind(block, axis, distance):
    devices = range(lax.axis_size(axis))
    route = [(i - distance, i) for i in devices if i - distance in devices]
    return lax.ppermute(block, axis, route)


def local(green, pair_index, pair_weight, phonon_offset, occupation, vertex, block_atoms):
    k_local = green.shape[0]
    e_local = green.shape[1]
    norb = green.shape[4]
    count_all = k_local * lax.axis_size("mom")
    picks = (
        pair_index[:, :, None] == jnp.arange(count_all, dtype=jnp.int32)[None, None, :]
    ).astype(jnp.float32)
    mixing = jnp.sum(picks * pair_weight[:, :, None], axis=1)
    spread = lax.all_to_all(green, "mom", split_axis=1, concat_axis=0, tiled=True)
    summed = jnp.dot(mixing, spread.reshape(count_all, -1), preferred_element_type=jnp.float32)
    summed = summed.reshape(spread.shape).astype(jnp.bfloat16)
    paired = lax.all_to_all(summed, "mom", split_axis=0, concat_axis=1, tiled=True)
    below = from_behind(paired, "en", 1)
    above = from_behind(paired, "en", -1)
    extended = jnp.concatenate([below[:, e_local - OFF_MAX :], paired, above[:, :OFF_MAX]], axis=1)
    group_size = 4
    halves = []
    rights = []
    for inner in range(group_size):
        shift_by = phonon_offset[inner]
        plus = lax.dynamic_slice_in_dim(extended, OFF_MAX + shift_by, e_local, 1).astype(
            jnp.float32
        )
        minus = lax.dynamic_slice_in_dim(extended, OFF_MAX - shift_by, e_local, 1).astype(
            jnp.float32
        )
        bose = occupation[inner]
        lesser = (bose + 1.0) * plus[:, :, :, 0] + bose * minus[:, :, :, 0]
        greater = bose * plus[:, :, :, 1] + (bose + 1.0) * minus[:, :, :, 1]
        source = jnp.stack([lesser, greater], axis=3).astype(jnp.bfloat16)
        left_block = vertex[inner][block_atoms[:, 0]]
        half = jnp.einsum(
            "bij,kebtjc->kebtic", left_block, source, preferred_element_type=jnp.float32
        )
        halves.append(half.astype(jnp.bfloat16).reshape(half.shape[:-1] + (2, norb)))
        rights.append(vertex[inner][block_atoms[:, 1]])
    stacked = jnp.stack(halves, axis=0)
    right_stack = jnp.stack(rights, axis=0)
    total = jnp.einsum(
        "mkebtipj,mblj->kebtipl", stacked, right_stack, preferred_element_type=jnp.float32
    )
    return total.reshape(green.shape).astype(jnp.bfloat16)


def solution(mesh):
    in_specs = (P("mom", "en", None, None, None, None), P(), P(), P(), P(), P(), P())
    out_specs = P("mom", "en", None, None, None, None)
    return jax.shard_map(local, mesh=mesh, in_specs=in_specs, out_specs=out_specs, check_vma=False)
```

profile of v0, /device:TPU:9, one launch (start us, length us, event | category | flops | bytes accessed | tf_op | source)
XLA Modules:
  0.0 80.9 jit_solution(660520852781302072)
XLA Ops:
  0.0 3.6 %all-to-all-start = ((bf16[1,8,2,2,64,128]{5,4,3,2,0,1:T(8,128)(2,1)}), bf16[1,8,2,2,64,128]{5,4,3,2,0,1:T(8,128)(2,1)S(1)}, u32[]{:S(2)}, u32[]{:S(2)}) async-start(bf16[1,8,2,2,64,128]{5,4,3,2,0,1:T(8,128)(2,1)} %bitcast.144), calls=%async_computation | async-start | bytes 1048576 | tf_op jit(solution)/shard_map/all_to_all | solution.py:24
  3.7 7.3 %all-to-all-done = bf16[1,8,2,2,64,128]{5,4,3,2,0,1:T(8,128)(2,1)S(1)} async-done(((bf16[1,8,2,2,64,128]{5,4,3,2,0,1:T(8,128)(2,1)}), bf16[1,8,2,2,64,128]{5,4,3,2,0,1:T(8,128)(2,1)S(1)}, u32[]{:S(2)}, u32[]{:S(2)}) %all-to-all-start) | async-done | bytes 524320 | tf_op jit(solution)/shard_map/all_to_all | solution.py:24
  11.8 0.9 %copy.45 = bf16[2,4,2,2,64,128]{5,4,3,2,1,0:T(8,128)(2,1)} copy(bf16[2,4,2,2,64,128]{5,0,4,3,2,1:T(2,128)(2,1)S(1)} %convolution_convert_fusion.4) | data formatting | bytes 1048576 | tf_op jit(solution)/shard_map/convert_element_type | solution.py:26
  12.8 3.6 %all-to-all-start.1 = ((bf16[2,4,2,2,64,128]{5,4,3,2,1,0:T(8,128)(2,1)}), bf16[2,4,2,2,64,128]{5,4,3,2,1,0:T(8,128)(2,1)S(1)}, u32[]{:S(2)}, u32[]{:S(2)}) async-start(bf16[2,4,2,2,64,128]{5,4,3,2,1,0:T(8,128)(2,1)} %copy.45), calls=%async_computation.1 | async-start | bytes 1048576 | tf_op jit(solution)/shard_map/all_to_all | solution.py:27
  16.6 6.2 %all-to-all-done.1 = bf16[2,4,2,2,64,128]{5,4,3,2,1,0:T(8,128)(2,1)S(1)} async-done(((bf16[2,4,2,2,64,128]{5,4,3,2,1,0:T(8,128)(2,1)}), bf16[2,4,2,2,64,128]{5,4,3,2,1,0:T(8,128)(2,1)S(1)}, u32[]{:S(2)}, u32[]{:S(2)}) %all-to-all-start.1) | async-done | bytes 524320 | tf_op jit(solution)/shard_map/all_to_all | solution.py:27
  22.9 5.5 %collective-permute-start = (bf16[1,8,2,2,64,128]{5,4,1,2,3,0:T(8,128)(2,1)S(1)}, bf16[1,8,2,2,64,128]{5,4,1,2,3,0:T(8,128)(2,1)S(1)}, u32[]{:S(2)}, u32[]{:S(2)}) collective-permute-start(bf16[1,8,2,2,64,128]{5,4,1,2,3,0:T(8,128)(2,1)S(1)} %copy.46), channel_id=1, source_target_pairs={{0,1},{1,2},{2,3},{3,4},{4,5},{5,6},{6,7},{7,8},{8,9},{9,10},{10,1... | collective-permute-start | bytes 1572872 | tf_op jit(solution)/shard_map/ppermute | solution.py:12
  28.4 1.9 %collective-permute-start.1 = (bf16[1,8,2,2,64,128]{5,4,1,2,3,0:T(8,128)(2,1)S(1)}, bf16[1,8,2,2,64,128]{5,4,1,2,3,0:T(8,128)(2,1)S(1)}, u32[]{:S(2)}, u32[]{:S(2)}) collective-permute-start(bf16[1,8,2,2,64,128]{5,4,1,2,3,0:T(8,128)(2,1)S(1)} %copy.46), channel_id=1, source_target_pairs={{1,0},{2,1},{3,2},{4,3},{5,4},{6,5},{7,6},{8,7},{9,8},{10,9},{11,1... | collective-permute-start | bytes 1572872 | tf_op jit(solution)/shard_map/ppermute | solution.py:12
  43.0 1.2 %gather_fusion.1 = bf16[2,64,64]{2,1,0:T(8,128)(2,1)} fusion(bf16[8,64,64]{2,1,0:T(8,128)(2,1)S(1)} %get-tuple-element.24, s32[1024]{0:T(1024)S(1)} %get-tuple-element.38), kind=kCustom, calls=%fused_computation.1 | custom fusion | bytes 32776 | tf_op jit(solution)/shard_map/gather | solution.py:51
  44.7 1.2 %gather_fusion.2 = bf16[2,64,64]{2,1,0:T(8,128)(2,1)} fusion(bf16[8,64,64]{2,1,0:T(8,128)(2,1)S(1)} %get-tuple-element.26, s32[1024]{0:T(1024)S(1)} %get-tuple-element.38), kind=kCustom, calls=%fused_computation.2 | custom fusion | bytes 32776 | tf_op jit(solution)/shard_map/gather | solution.py:51
  46.4 1.2 %gather_fusion.3 = bf16[2,64,64]{2,1,0:T(8,128)(2,1)} fusion(bf16[8,64,64]{2,1,0:T(8,128)(2,1)S(1)} %get-tuple-element.25, s32[1024]{0:T(1024)S(1)} %get-tuple-element.38), kind=kCustom, calls=%fused_computation.3 | custom fusion | bytes 32776 | tf_op jit(solution)/shard_map/gather | solution.py:51
  51.1 2.3 %dynamic-slice_convert_fusion.7 = (f32[1,8,2,2,64,128]{5,4,1,2,3,0:T(8,128)S(1)}, f32[1,8,2,2,64,128]{5,4,1,2,3,0:T(8,128)S(1)}, f32[1,8,2,2,64,128]{5,4,1,2,3,0...) fusion(bf16[1,16,2,2,64,128]{5,4,1,2,3,0:T(8,128)(2,1)S(1)} %pa, ...), kind=kLoop, calls=%fused_computation.75 | loop fusion | flops 2097152 | bytes 12582944 | tf_op jit(solution)/shard_map/convert_element_type | solution.py:36
  53.3 0.9 %fusion.33 = (bf16[8,2,1,64,128]{4,3,2,0,1:T(8,128)(2,1)S(1)}, bf16[8,2,1,64,128]{4,3,2,0,1:T(8,128)(2,1)S(1)}) fusion(f32[1,8,2,2,64,128]{5,4,1,2,3,0:T(8,128)S(1)} %get-tuple-element.22, f32[1,8,2,2,64,128]{5,4,1,2,3,0:T(8,128)S(1)} %get-tuple-element.15, f32[]{:T(128)} %bitcast.10, f32[]{:T(128)S(6)} %add.159), kind=kLoop, calls=%fused_computation.76 | loop fusion | flops 1048576 | bytes 2621448 | tf_op jit(solution)/shard_map/stack | solution.py:45
  54.2 1.1 %fusion.7 = bf16[1,8,2,2,64,128]{5,4,3,1,2,0:T(8,128)(2,1)} fusion(bf16[8,2,1,64,128]{4,3,2,0,1:T(8,128)(2,1)S(1)} %get-tuple-element.8, bf16[8,2,1,64,128]{4,3,2,0,1:T(8,128)(2,1)S(1)} %get-tuple-element.7, bf16[2,64,64]{2,1,0:T(8,128)(2,1)S(1)} %gather_fusion.4), kind=kOutput, calls=%fused_computation.22 | convolution fusion | flops 34865152 | bytes 1064960 | tf_op jit(solution)/shard_map/bij,kebtjc->kebtic/dot_general | solution.py:47
  55.3 3.2 %stack_reshape.12 = bf16[1,1,8,2,2,64,2,64]{7,6,5,4,2,3,1,0:T(2,128)(2,1)} reshape(bf16[1,8,2,2,64,128]{5,4,3,1,2,0:T(8,128)(2,1)} %fusion.7) | data formatting | bytes 1048576 | tf_op jit(solution)/shard_map/stack;reshape | solution.py:52
  58.5 2.6 %copy.53 = bf16[1,1,8,2,2,64,2,64]{7,5,0,6,4,2,3,1:T(8,128)(2,1)} copy(bf16[1,1,8,2,2,64,2,64]{7,6,5,4,2,3,1,0:T(2,128)(2,1)} %stack_reshape.12) | data formatting | bytes 1048576 | tf_op jit(solution)/shard_map/stack;reshape | solution.py:52
  61.1 3.7 %fusion.35 = (bf16[8,2,1,64,128]{4,3,0,1,2:T(8,128)(2,1)S(1)}, bf16[8,2,1,64,128]{4,3,0,1,2:T(8,128)(2,1)S(1)}, bf16[8,2,1,64,128]{4,3,0,1,2:T(8,128)(2,1)S(1)}, bf16[8,2,1,64,128]{4,3,0,1,2:T(8,128)(2,1)}) fusion(f32[1,8,2,2,64,128]{5,4,1,2,3,0:T(8,128)S(1)} %copy-done.1, f32[1,8,2,2,64,128]{5,4,1,2,3,0:T(8,128)} %get-tuple-element.21, f32[]{:T(128)} %bitcast.28, ...), kind=kLoop, calls=%fused_computation.78 | loop fusion | flops 2097152 | bytes 5242896 | tf_op jit(solution)/shard_map/stack | solution.py:45
  64.8 1.1 %fusion.8 = bf16[1,8,2,2,64,128]{5,4,3,1,2,0:T(8,128)(2,1)} fusion(bf16[2,64,64]{2,1,0:T(8,128)(2,1)S(1)} %gather_fusion.5, bf16[8,2,1,64,128]{4,3,0,1,2:T(8,128)(2,1)S(1)} %get-tuple-element.10, bf16[8,2,1,64,128]{4,3,0,1,2:T(8,128)(2,1)S(1)} %get-tuple-element.9), kind=kOutput, calls=%fused_computation.23 | convolution fusion | flops 34078720 | bytes 1064960 | tf_op jit(solution)/shard_map/bij,kebtjc->kebtic/dot_general | solution.py:47
  65.8 2.4 %stack_reshape.13 = bf16[1,1,8,2,2,64,2,64]{7,6,5,4,2,3,1,0:T(2,128)(2,1)S(1)} reshape(bf16[1,8,2,2,64,128]{5,4,3,1,2,0:T(8,128)(2,1)} %fusion.8) | data formatting | bytes 1048576 | tf_op jit(solution)/shard_map/stack;reshape | solution.py:52
  68.3 1.3 %copy.54 = bf16[1,1,8,2,2,64,2,64]{7,5,0,6,4,2,3,1:T(8,128)(2,1)} copy(bf16[1,1,8,2,2,64,2,64]{7,6,5,4,2,3,1,0:T(2,128)(2,1)S(1)} %stack_reshape.13) | data formatting | bytes 1048576 | tf_op jit(solution)/shard_map/stack;reshape | solution.py:52
  69.6 1.1 %fusion.9 = bf16[1,8,2,2,64,128]{5,4,3,1,2,0:T(8,128)(2,1)} fusion(bf16[2,64,64]{2,1,0:T(8,128)(2,1)S(1)} %gather_fusion.6, bf16[8,2,1,64,128]{4,3,0,1,2:T(8,128)(2,1)S(1)} %get-tuple-element.35, bf16[8,2,1,64,128]{4,3,0,1,2:T(8,128)(2,1)S(1)} %copy-done.5), kind=kOutput, calls=%fused_computation.24 | convolution fusion | flops 34078720 | bytes 1064960 | tf_op jit(solution)/shard_map/bij,kebtjc->kebtic/dot_general | solution.py:47
  70.6 2.4 %stack_reshape.14 = bf16[1,1,8,2,2,64,2,64]{7,6,5,4,2,3,1,0:T(2,128)(2,1)S(1)} reshape(bf16[1,8,2,2,64,128]{5,4,3,1,2,0:T(8,128)(2,1)} %fusion.9) | data formatting | bytes 1048576 | tf_op jit(solution)/shard_map/stack;reshape | solution.py:52
  73.1 1.3 %copy.55 = bf16[1,1,8,2,2,64,2,64]{7,5,0,6,4,2,3,1:T(8,128)(2,1)} copy(bf16[1,1,8,2,2,64,2,64]{7,6,5,4,2,3,1,0:T(2,128)(2,1)S(1)} %stack_reshape.14) | data formatting | bytes 1048576 | tf_op jit(solution)/shard_map/stack;reshape | solution.py:52
  77.5 2.3 %bitcast_convert_fusion = bf16[2,64,8,2,64,2]{4,1,5,3,2,0:T(8,128)(2,1)S(1)} fusion(bf16[1,1,8,2,2,64,2,64]{7,5,0,6,4,2,3,1:T(8,128)(2,1)S(1)} %copy.56, bf16[1,1,8,2,2,64,2,64]{7,5,0,6,4,2,3,1:T(8,128)(2,1)S(1)} %copy-done.4, bf16[1,1,8,2,2,64,2,64]{7,5,0,6,4,2,3,1:T(8,128)(2,1)S(1)} %copy-done.3, bf16[1,1,8,2,2,64,2,64]{7,5,0,6,4,2,3,1:T(8,128)(2,1)S(1)} %copy-done.2, ...), kind=kOutput, calls=%fused_computation.16 | convolution fusion | flops 143130624 | bytes 2686976 | tf_op jit(solution)/shard_map/mkebtipj,mblj->kebtipl/dot_general | solution.py:54
  79.8 1.1 %copy.57 = bf16[1,8,2,2,64,128]{5,4,3,2,1,0:T(8,128)(2,1)} copy(bf16[1,8,2,2,64,128]{4,5,3,1,2,0:T(8,128)(2,1)S(1)} %bitcast.143) | data formatting | bytes 1048576 | tf_op jit(solution)/shard_map/convert_element_type | solution.py:57
  (53 shorter events, 8.5 us)
Async XLA Ops:
  0.0 3.6 %copy-start.14 = (s32[2,4]{1,0:T(2,128)S(1)}, s32[2,4]{1,0:T(2,128)}, u32[]{:S(2)}) copy-start(s32[2,4]{1,0:T(2,128)} %param.8) | copy-start | bytes 100
  0.0 3.6 %copy-start.13 = (f32[2,4]{1,0:T(2,128)S(1)}, f32[2,4]{1,0:T(2,128)}, u32[]{:S(2)}) copy-start(f32[2,4]{1,0:T(2,128)} %param.9) | copy-start | bytes 100
  0.0 11.0 %all-to-all-start = ((bf16[1,8,2,2,64,128]{5,4,3,2,0,1:T(8,128)(2,1)}), bf16[1,8,2,2,64,128]{5,4,3,2,0,1:T(8,128)(2,1)S(1)}, u32[]{:S(2)}, u32[]{:S(2)}) async-start(bf16[1,8,2,2,64,128]{5,4,3,2,0,1:T(8,128)(2,1)} %bitcast.144), calls=%async_computation | async-start | bytes 1048576 | tf_op jit(solution)/shard_map/all_to_all | solution.py:24
  11.8 4.6 %copy-start.12 = (s32[2,2]{1,0:T(2,128)S(1)}, s32[2,2]{1,0:T(2,128)}, u32[]{:S(2)}) copy-start(s32[2,2]{1,0:T(2,128)} %param.13) | copy-start | bytes 52
  12.8 17.6 %copy-start.10 = (s32[4]{0:T(128)S(1)}, s32[4]{0:T(128)}, u32[]{:S(2)}) copy-start(s32[4]{0:T(128)} %param.10) | copy-start | bytes 52
  12.8 28.5 %copy-start.6 = (bf16[4,8,64,64]{3,2,1,0:T(8,128)(2,1)S(1)}, bf16[4,8,64,64]{3,2,1,0:T(8,128)(2,1)}, u32[]{:S(2)}) copy-start(bf16[4,8,64,64]{3,2,1,0:T(8,128)(2,1)} %param.12) | copy-start | bytes 786436
  12.8 10.1 %all-to-all-start.1 = ((bf16[2,4,2,2,64,128]{5,4,3,2,1,0:T(8,128)(2,1)}), bf16[2,4,2,2,64,128]{5,4,3,2,1,0:T(8,128)(2,1)S(1)}, u32[]{:S(2)}, u32[]{:S(2)}) async-start(bf16[2,4,2,2,64,128]{5,4,3,2,1,0:T(8,128)(2,1)} %copy.45), calls=%async_computation.1 | async-start | bytes 1048576 | tf_op jit(solution)/shard_map/all_to_all | solution.py:27
  22.9 24.7 %copy-start.11 = (f32[4]{0:T(128)S(1)}, f32[4]{0:T(128)}, u32[]{:S(2)}) copy-start(f32[4]{0:T(128)} %param.11) | copy-start | bytes 52
  22.9 28.0 %collective-permute-start = (bf16[1,8,2,2,64,128]{5,4,1,2,3,0:T(8,128)(2,1)S(1)}, bf16[1,8,2,2,64,128]{5,4,1,2,3,0:T(8,128)(2,1)S(1)}, u32[]{:S(2)}, u32[]{:S(2)}) collective-permute-start(bf16[1,8,2,2,64,128]{5,4,1,2,3,0:T(8,128)(2,1)S(1)} %copy.46), channel_id=1, source_target_pairs={{0,1},{1,2},{2,3},{3,4},{4,5},{5,6},{6,7},{7,8},{8,9},{9,10},{10,1... | collective-permute-start | bytes 1572872 | tf_op jit(solution)/shard_map/ppermute | solution.py:12
  28.4 22.5 %collective-permute-start.1 = (bf16[1,8,2,2,64,128]{5,4,1,2,3,0:T(8,128)(2,1)S(1)}, bf16[1,8,2,2,64,128]{5,4,1,2,3,0:T(8,128)(2,1)S(1)}, u32[]{:S(2)}, u32[]{:S(2)}) collective-permute-start(bf16[1,8,2,2,64,128]{5,4,1,2,3,0:T(8,128)(2,1)S(1)} %copy.46), channel_id=1, source_target_pairs={{1,0},{2,1},{3,2},{4,3},{5,4},{6,5},{7,6},{8,7},{9,8},{10,9},{11,1... | collective-permute-start | bytes 1572872 | tf_op jit(solution)/shard_map/ppermute | solution.py:12
  58.5 2.6 %copy-start = (f32[1,8,2,2,64,128]{5,4,1,2,3,0:T(8,128)S(1)}, f32[1,8,2,2,64,128]{5,4,1,2,3,0:T(8,128)}, u32[]{:S(2)}) copy-start(f32[1,8,2,2,64,128]{5,4,1,2,3,0:T(8,128)} %get-tuple-element.19) | copy-start | bytes 3145732
  58.5 2.6 %copy-start.1 = (f32[1,8,2,2,64,128]{5,4,1,2,3,0:T(8,128)S(1)}, f32[1,8,2,2,64,128]{5,4,1,2,3,0:T(8,128)}, u32[]{:S(2)}) copy-start(f32[1,8,2,2,64,128]{5,4,1,2,3,0:T(8,128)} %get-tuple-element.20) | copy-start | bytes 3145732
  68.3 1.3 %copy-start.5 = (bf16[8,2,1,64,128]{4,3,0,1,2:T(8,128)(2,1)S(1)}, bf16[8,2,1,64,128]{4,3,0,1,2:T(8,128)(2,1)}, u32[]{:S(2)}) copy-start(bf16[8,2,1,64,128]{4,3,0,1,2:T(8,128)(2,1)} %get-tuple-element.36) | copy-start | bytes 786436
  75.4 1.2 %copy-start.4 = (bf16[1,1,8,2,2,64,2,64]{7,5,0,6,4,2,3,1:T(8,128)(2,1)S(1)}, bf16[1,1,8,2,2,64,2,64]{7,5,0,6,4,2,3,1:T(8,128)(2,1)}, u32[]{:S(2)}) copy-start(bf16[1,1,8,2,2,64,2,64]{7,5,0,6,4,2,3,1:T(8,128)(2,1)} %copy.55) | copy-start | bytes 1572868
  75.5 1.2 %copy-start.7 = (bf16[2,64,64]{2,1,0:T(8,128)(2,1)S(1)}, bf16[2,64,64]{2,1,0:T(8,128)(2,1)}, u32[]{:S(2)}) copy-start(bf16[2,64,64]{2,1,0:T(8,128)(2,1)} %gather_fusion.1) | copy-start | bytes 49156
  75.5 1.2 %copy-start.8 = (bf16[2,64,64]{2,1,0:T(8,128)(2,1)S(1)}, bf16[2,64,64]{2,1,0:T(8,128)(2,1)}, u32[]{:S(2)}) copy-start(bf16[2,64,64]{2,1,0:T(8,128)(2,1)} %gather_fusion.2) | copy-start | bytes 49156
  75.5 1.2 %copy-start.9 = (bf16[2,64,64]{2,1,0:T(8,128)(2,1)S(1)}, bf16[2,64,64]{2,1,0:T(8,128)(2,1)}, u32[]{:S(2)}) copy-start(bf16[2,64,64]{2,1,0:T(8,128)(2,1)} %gather_fusion.3) | copy-start | bytes 49156
  75.9 1.3 %copy-start.2 = (bf16[1,1,8,2,2,64,2,64]{7,5,0,6,4,2,3,1:T(8,128)(2,1)S(1)}, bf16[1,1,8,2,2,64,2,64]{7,5,0,6,4,2,3,1:T(8,128)(2,1)}, u32[]{:S(2)}) copy-start(bf16[1,1,8,2,2,64,2,64]{7,5,0,6,4,2,3,1:T(8,128)(2,1)} %copy.53) | copy-start | bytes 1572868
  75.9 1.6 %copy-start.3 = (bf16[1,1,8,2,2,64,2,64]{7,5,0,6,4,2,3,1:T(8,128)(2,1)S(1)}, bf16[1,1,8,2,2,64,2,64]{7,5,0,6,4,2,3,1:T(8,128)(2,1)}, u32[]{:S(2)}) copy-start(bf16[1,1,8,2,2,64,2,64]{7,5,0,6,4,2,3,1:T(8,128)(2,1)} %copy.54) | copy-start | bytes 1572868
where the time goes:
time: 82.3 us; the launch traced here: 80.9 us
  local copies, waits for them, and re-layouts  25.1 us (30%)
  starting transfers between devices  14.7 us (18%)
  waiting for transfers between devices  13.5 us (16%)
  between operations  13.2 us (16%)
  other arithmetic  7.99 us (10%)
  matrix products  6.45 us (8%)
    another operation x8, local copies, waits for them, and re-layouts, local(): stacked = jnp.stack(halves, axis=0)  13.8 us
    ppermute x2, starting transfers between devices, from_behind(): return lax.ppermute(block, axis, route)  7.43 us
    all_to_all x1, waiting for transfers between devices, local(): lax.all_to_all(green, 'mom', split_axis=1, concat_axis=0, tiled=True)  7.26 us
    all_to_all x1, waiting for transfers between devices, local(): lax.all_to_all(summed, 'mom', split_axis=0, concat_axis=1, tiled=True)  6.24 us
    another operation x3, other arithmetic, local(): source = jnp.stack([lesser, greater], axis=3).astype(jnp.bfloat16)  5.36 us
    gather x4, local copies, waits for them, and re-layouts, local(): rights.append(vertex[inner][block_atoms[:, 1]])  4.04 us
    all_to_all x1, starting transfers between devices, local(): lax.all_to_all(summed, 'mom', split_axis=0, concat_axis=1, tiled=True)  3.62 us
    all_to_all x1, starting transfers between devices, local(): lax.all_to_all(green, 'mom', split_axis=1, concat_axis=0, tiled=True)  3.62 us
  transfers between devices with their start and end apart: 4, of which 2 were waited for; matrix products, arithmetic and copies ran while one was open for 10% of the time, Pallas kernels for 0%

commit v1 on v0

v1 whole, which is shorter than its diff:
```python
import functools

import jax
import jax.numpy as jnp
from jax import lax
from jax.experimental import pallas as pl
from jax.experimental.pallas import tpu as pltpu
from jax.sharding import PartitionSpec as P

OFF_MAX = 4
MESH = pl.DeviceIdType.MESH


def kernel(
    n_mom,
    n_en,
    green,
    vertex,
    pair_index,
    pair_weight,
    offset,
    occupation,
    atoms,
    out,
    own,
    got,
    verts,
    left_w,
    right_w,
    result,
    x_send,
    x_recv,
    h_send,
    h_recv,
    local_sem,
    out_sem,
    *ext,
):
    e_local, blocks = green.shape[1], green.shape[2]
    norb = green.shape[4]
    modes = vertex.shape[0]
    pairs = pair_index.shape[1]
    chunks = 2 * blocks
    half = e_local // 2
    me_k, me_e = lax.axis_index("mom"), lax.axis_index("en")
    odd = lax.rem(me_e, 2)
    starts = (odd * half, half - odd * half)
    peers = (me_e - 1 + 2 * odd, me_e + 1 - 2 * odd)
    there = tuple(jnp.logical_and(p >= 0, p < n_en) for p in peers)
    low_edge, high_edge = OFF_MAX, e_local
    send_from = (low_edge + odd * (high_edge - low_edge), high_edge - odd * (high_edge - low_edge))
    mine_at = (odd * (OFF_MAX + e_local), (1 - odd) * (OFF_MAX + e_local))
    peer_at = ((1 - odd) * (OFF_MAX + e_local), odd * (OFF_MAX + e_local))

    barrier = pltpu.get_barrier_semaphore()
    for d in range(1, n_mom):
        pl.semaphore_signal(
            barrier, inc=1, device_id={"mom": lax.rem(me_k + d, n_mom)}, device_id_type=MESH
        )
    for ph in range(2):

        @pl.when(there[ph])
        def _():
            pl.semaphore_signal(barrier, inc=1, device_id={"en": peers[ph]}, device_id_type=MESH)

    met = sum((t.astype(jnp.int32) for t in there), jnp.int32(n_mom - 1))
    pl.semaphore_wait(barrier, met)

    def cross(ph, c, d):
        b, t = divmod(c, 2)
        es = pl.ds(starts[ph], half)
        return pltpu.make_async_remote_copy(
            src_ref=green.at[0, es, b, t],
            dst_ref=got.at[d - 1, c, es],
            send_sem=x_send.at[ph, c, d - 1],
            recv_sem=x_recv.at[ph, c, d - 1],
            device_id={"mom": lax.rem(me_k + d, n_mom)},
            device_id_type=MESH,
        )

    def halo(ph, c):
        return pltpu.make_async_remote_copy(
            src_ref=ext[c].at[pl.ds(send_from[ph], OFF_MAX)],
            dst_ref=ext[c].at[pl.ds(peer_at[ph], OFF_MAX)],
            send_sem=h_send.at[ph, c],
            recv_sem=h_recv.at[ph, c],
            device_id={"en": peers[ph]},
            device_id_type=MESH,
        )

    for ph in range(2):
        for c in range(chunks):
            for d in range(1, n_mom):
                cross(ph, c, d).start()
    get_own = pltpu.make_async_copy(green.at[0], own, local_sem.at[0])
    get_own.start()
    get_verts = pltpu.make_async_copy(vertex, verts, local_sem.at[1])
    get_verts.start()

    def share(q):
        total = jnp.float32(0.0)
        for j in range(pairs):
            total += jnp.where(pair_index[me_k, j] == q, pair_weight[me_k, j], jnp.float32(0.0))
        return total

    shares = [share(lax.rem(me_k - d + n_mom, n_mom)) for d in range(n_mom)]

    for ph in range(2):

        @pl.when(jnp.logical_not(there[ph]))
        def _():
            for c in range(chunks):
                ext[c][pl.ds(mine_at[ph], OFF_MAX)] = jnp.zeros(
                    (OFF_MAX, norb, 2 * norb), jnp.bfloat16
                )

    get_verts.wait()
    none = jnp.zeros((norb, norb), jnp.float32)
    for b in range(blocks):
        for m in range(modes):
            left_w[b, m] = verts[m, atoms[b, 0]]
            turned = verts[m, atoms[b, 1]].astype(jnp.float32).T
            right_w[b, pl.ds(2 * m * norb, norb)] = jnp.concatenate([turned, none], axis=1).astype(
                jnp.bfloat16
            )
            right_w[b, pl.ds((2 * m + 1) * norb, norb)] = jnp.concatenate(
                [none, turned], axis=1
            ).astype(jnp.bfloat16)
    get_own.wait()

    def pair_sum(ph, c):
        b, t = divmod(c, 2)
        es = pl.ds(starts[ph], half)
        total = shares[0] * own[es, b, t].astype(jnp.float32)
        for d in range(1, n_mom):
            cross(ph, c, d).wait_recv()
            total += shares[d] * got[d - 1, c, es].astype(jnp.float32)
        ext[c][pl.ds(OFF_MAX + starts[ph], half)] = total.astype(jnp.bfloat16)

        @pl.when(there[ph])
        def _():
            halo(ph, c).start()

    def store(c):
        b, t = divmod(c, 2)
        return pltpu.make_async_copy(result.at[c], out.at[0, :, b, t], out_sem.at[c])

    def compute(c):
        b, t = divmod(c, 2)
        for ph in range(2):

            @pl.when(there[ph])
            def _():
                halo(ph, c).wait_recv()

        lefts = []
        for m in range(modes):
            w, bose = offset[m], occupation[m]
            up, down = (bose + 1.0, bose) if t == 0 else (bose, bose + 1.0)
            plus = ext[c][pl.ds(OFF_MAX + w, e_local)].astype(jnp.float32)
            minus = ext[c][pl.ds(OFF_MAX - w, e_local)].astype(jnp.float32)
            source = (up * plus + down * minus).astype(jnp.bfloat16)
            wide = jnp.concatenate([source[e] for e in range(e_local)], axis=1)
            lefts.append(
                jnp.dot(left_w[b, m], wide, preferred_element_type=jnp.float32).astype(jnp.bfloat16)
            )
        tall = jnp.concatenate(
            [
                jnp.concatenate([x[:, 2 * norb * e : 2 * norb * (e + 1)] for x in lefts], axis=1)
                for e in range(e_local)
            ],
            axis=0,
        )
        total = jnp.dot(tall, right_w[b], preferred_element_type=jnp.float32)
        result[c] = total.astype(jnp.bfloat16).reshape(e_local, norb, 2 * norb)
        store(c).start()

    for c in range(chunks):
        pair_sum(0, c)
    for c in range(chunks):
        pair_sum(1, c)
        if c > 0:
            compute(c - 1)
    compute(chunks - 1)

    for ph in range(2):
        for c in range(chunks):
            for d in range(1, n_mom):
                cross(ph, c, d).wait_send()

        @pl.when(there[ph])
        def _():
            for c in range(chunks):
                halo(ph, c).wait_send()

    for c in range(chunks):
        store(c).wait()


def local(n_mom, n_en, green, pair_index, pair_weight, offset, occupation, vertex, atoms):
    _, e_local, blocks, _, norb, _ = green.shape
    modes = vertex.shape[0]
    chunks = 2 * blocks
    tile = (norb, 2 * norb)
    slots = max(n_mom - 1, 1)
    bf16 = jnp.bfloat16
    hbm = pl.BlockSpec(memory_space=pl.ANY)
    smem = pl.BlockSpec(memory_space=pltpu.SMEM)
    dma = pltpu.SemaphoreType.DMA
    flops = 2 * e_local * chunks * modes * norb * norb * 4 * norb
    return pl.pallas_call(
        functools.partial(kernel, n_mom, n_en),
        out_shape=jax.ShapeDtypeStruct(green.shape, bf16),
        in_specs=[hbm, hbm, smem, smem, smem, smem, smem],
        out_specs=hbm,
        scratch_shapes=[
            pltpu.VMEM(green.shape[1:], bf16),
            pltpu.VMEM((slots, chunks, e_local) + tile, bf16),
            pltpu.VMEM(vertex.shape, bf16),
            pltpu.VMEM((blocks, modes, norb, norb), bf16),
            pltpu.VMEM((blocks, 2 * modes * norb, 2 * norb), bf16),
            pltpu.VMEM((chunks, e_local) + tile, bf16),
            dma((2, chunks, slots)),
            dma((2, chunks, slots)),
            dma((2, chunks)),
            dma((2, chunks)),
            dma((2,)),
            dma((chunks,)),
        ]
        + [pltpu.VMEM((e_local + 2 * OFF_MAX,) + tile, bf16) for _ in range(chunks)],
        compiler_params=pltpu.CompilerParams(
            collective_id=0, has_side_effects=True, vmem_limit_bytes=60 * 2**20
        ),
        cost_estimate=pl.CostEstimate(
            flops=flops, bytes_accessed=4 * green.size, transcendentals=0
        ),
    )(green, vertex, pair_index, pair_weight, offset, occupation, atoms)


def solution(mesh):
    spec = P("mom", "en", None, None, None, None)
    body = functools.partial(local, mesh.shape["mom"], mesh.shape["en"])
    return jax.shard_map(
        body, mesh=mesh, in_specs=(spec,) + (P(),) * 6, out_specs=spec, check_vma=False
    )
```

time: 82.3 us -> 21.1 us (0.26); the launches traced: 80.9 us -> 20.9 us
  local copies, waits for them, and re-layouts: 25.1 us -> 1.88 us
  Pallas kernels: 0 us -> 19 us
  starting transfers between devices: 14.7 us -> 0 us
  waiting for transfers between devices: 13.5 us -> 0 us
  between operations: 13.2 us -> 0.01 us
  other arithmetic: 7.99 us -> 0 us
  matrix products: 6.45 us -> 0 us
    pallas_call x0 -> x1, Pallas kernels: none -> 19 us  [local(): pl.pallas_call(functools.partial(kernel, n_mom, n_en), out_shape=jax.Shap...]
    another operation x8 -> x0, local copies, waits for them, and re-layouts: 13.8 us -> none  [local(): stacked = jnp.stack(halves, axis=0)]
    all_to_all x2 -> x0, waiting for transfers between devices: 13.5 us -> none  [the longest x1 7.26 us: local(): lax.all_to_all(green, 'mom', split_axis=1, concat_axis=0, tiled=True)]
    ppermute x2 -> x0, starting transfers between devices: 7.43 us -> none  [from_behind(): return lax.ppermute(block, axis, route)]
    all_to_all x2 -> x0, starting transfers between devices: 7.24 us -> none  [the longest x1 3.62 us: local(): lax.all_to_all(summed, 'mom', split_axis=0, concat_axis=1, tiled=True)]
    dot_general x6 -> x0, matrix products: 6.45 us -> none  [the longest x4 3.51 us: local(): jnp.einsum('bij,kebtjc->kebtic', left_block, source, preferred_element_ty...]
    gather x8 -> x0, local copies, waits for them, and re-layouts: 6.27 us -> none  [the longest x4 4.04 us: local(): rights.append(vertex[inner][block_atoms[:, 1]])]
    another operation x3 -> x0, other arithmetic: 5.36 us -> none  [local(): source = jnp.stack([lesser, greater], axis=3).astype(jnp.bfloat16)]
  transfers between devices with their start and end apart: 4 -> 0, of which waited for: 2 -> 0; matrix products, arithmetic and copies ran while one was open for 10% -> 0% of each run, Pallas kernels for 0% -> 0%
where the time goes in v1:
time: 21.1 us; the launch traced here: 20.9 us
  Pallas kernels  19 us (90%)
  local copies, waits for them, and re-layouts  1.88 us (9%)
    pallas_call x1, Pallas kernels, local(): pl.pallas_call(functools.partial(kernel, n_mom, n_en), out_shape=jax.Shap...  19 us
    unnamed x1, local copies, waits for them, and re-layouts  1.88 us

profile of v1, /device:TPU:9, one launch (start us, length us, event | category | flops | bytes accessed | tf_op | source)
XLA Modules:
  0.0 20.9 jit_solution(8530756879360195320)
XLA Ops:
  0.0 19.0 %shard_map.73 = bf16[1,8,2,2,64,128]{5,4,3,2,1,0:T(8,128)(2,1)} custom-call(bf16[1,8,2,2,64,128]{5,4,3,2,1,0:T(8,128)(2,1)} %green.1, bf16[4,8,64,64]{3,2,1,0:T(8,128)(2,1)} %vertex.1, s32[2,4]{1,0:T(2,128)} %pair_index.1, f32[2,4]{1,0:T(2,128)} %pair_weight.1, s32[4]{0:T(128)} %offset.1, f32[4]{0:T(128)} %occupation.1, s32[2,2]{1,0:T(2,128)} %atoms.1), custom_call_target="tpu_custom_call" | custom-call | flops 268435456 | bytes 1048576 | tf_op jit(solution)/shard_map/pallas_call | solution.py:211
  19.0 1.9 %copy.9 = bf16[1,8,2,2,64,128]{5,4,3,2,1,0:T(8,128)(2,1)} copy(bf16[1,8,2,2,64,128]{5,4,3,2,1,0:T(8,128)(2,1)} %shard_map.73) | data formatting | bytes 1048576

commit v2 on v1

--- a/solution.py
+++ b/solution.py
@@ -16,12 +16,17 @@
     n_en,
     green,
     vertex,
+    pair_index_in,
+    pair_weight_in,
+    offset_in,
+    occupation_in,
+    atoms_in,
+    out,
     pair_index,
     pair_weight,
     offset,
     occupation,
     atoms,
-    out,
     own,
     got,
     verts,
@@ -39,7 +44,7 @@
     e_local, blocks = green.shape[1], green.shape[2]
     norb = green.shape[4]
     modes = vertex.shape[0]
-    pairs = pair_index.shape[1]
+    pairs = pair_index_in.shape[1]
     chunks = 2 * blocks
     half = e_local // 2
     me_k, me_e = lax.axis_index("mom"), lax.axis_index("en")
@@ -92,10 +97,25 @@
         for c in range(chunks):
             for d in range(1, n_mom):
                 cross(ph, c, d).start()
+    smalls = (
+        (pair_index_in, pair_index),
+        (pair_weight_in, pair_weight),
+        (offset_in, offset),
+        (occupation_in, occupation),
+        (atoms_in, atoms),
+    )
+    gets = [
+        pltpu.make_async_copy(src, dst, local_sem.at[2 + i]) for i, (src, dst) in enumerate(smalls)
+    ]
+    for get in gets:
+        get.start()
     get_own = pltpu.make_async_copy(green.at[0], own, local_sem.at[0])
     get_own.start()
     get_verts = pltpu.make_async_copy(vertex, verts, local_sem.at[1])
     get_verts.start()
+
+    for get in gets:
+        get.wait()
 
     def share(q):
         total = jnp.float32(0.0)
@@ -205,15 +225,16 @@
     slots = max(n_mom - 1, 1)
     bf16 = jnp.bfloat16
     hbm = pl.BlockSpec(memory_space=pl.ANY)
-    smem = pl.BlockSpec(memory_space=pltpu.SMEM)
+    small = (pair_index, pair_weight, offset, occupation, atoms)
     dma = pltpu.SemaphoreType.DMA
     flops = 2 * e_local * chunks * modes * norb * norb * 4 * norb
     return pl.pallas_call(
         functools.partial(kernel, n_mom, n_en),
         out_shape=jax.ShapeDtypeStruct(green.shape, bf16),
-        in_specs=[hbm, hbm, smem, smem, smem, smem, smem],
+        in_specs=[hbm] * 7,
         out_specs=hbm,
-        scratch_shapes=[
+        scratch_shapes=[pltpu.SMEM(x.shape, x.dtype) for x in small]
+        + [
             pltpu.VMEM(green.shape[1:], bf16),
             pltpu.VMEM((slots, chunks, e_local) + tile, bf16),
             pltpu.VMEM(vertex.shape, bf16),
@@ -224,7 +245,7 @@
             dma((2, chunks, slots)),
             dma((2, chunks)),
             dma((2, chunks)),
-            dma((2,)),
+            dma((2 + len(small),)),
             dma((chunks,)),
         ]
         + [pltpu.VMEM((e_local + 2 * OFF_MAX,) + tile, bf16) for _ in range(chunks)],

time: 21.1 us -> 20.3 us (0.962)
  Pallas kernels: 19 us -> 18.3 us
    pallas_call x1, Pallas kernels: 19 us -> 18.3 us  [local(): pl.pallas_call(functools.partial(kernel, n_mom, n_en), out_shape=jax.Shap...]
where the time goes in v2:
time: 20.3 us; the launch traced here: 20.2 us
  Pallas kernels  18.3 us (90%)
  local copies, waits for them, and re-layouts  1.88 us (9%)
    pallas_call x1, Pallas kernels, local(): pl.pallas_call(functools.partial(kernel, n_mom, n_en), out_shape=jax.Shap...  18.3 us
    unnamed x1, local copies, waits for them, and re-layouts  1.88 us

profile of v2, /device:TPU:9, one launch (start us, length us, event | category | flops | bytes accessed | tf_op | source)
XLA Modules:
  0.0 20.2 jit_solution(5308328187616485745)
XLA Ops:
  0.0 18.3 %shard_map.73 = bf16[1,8,2,2,64,128]{5,4,3,2,1,0:T(8,128)(2,1)} custom-call(bf16[1,8,2,2,64,128]{5,4,3,2,1,0:T(8,128)(2,1)} %green.1, bf16[4,8,64,64]{3,2,1,0:T(8,128)(2,1)} %vertex.1, s32[2,4]{1,0:T(2,128)} %pair_index_in.1, f32[2,4]{1,0:T(2,128)} %pair_weight_in.1, s32[4]{0:T(128)} %offset_in.1, f32[4]{0:T(128)} %occupation_in.1, s32[2,2]{1,0:T(2,128)} %atoms_in.1), custom_call_target="tpu_custom_call" | custom-call | flops 268435456 | bytes 1048576 | tf_op jit(solution)/shard_map/pallas_call | solution.py:231
  18.3 1.9 %copy.9 = bf16[1,8,2,2,64,128]{5,4,3,2,1,0:T(8,128)(2,1)} copy(bf16[1,8,2,2,64,128]{5,4,3,2,1,0:T(8,128)(2,1)} %shard_map.73) | data formatting | bytes 1048576

commit v3 on v2

--- a/solution.py
+++ b/solution.py
@@ -163,7 +163,7 @@
 
     def store(c):
         b, t = divmod(c, 2)
-        return pltpu.make_async_copy(result.at[c], out.at[0, :, b, t], out_sem.at[c])
+        return pltpu.make_async_copy(result.at[c], out.at[c], out_sem.at[c])
 
     def compute(c):
         b, t = divmod(c, 2)
@@ -217,6 +217,21 @@
         store(c).wait()
 
 
+def deliver(made, out, held, get_sem, put_sem):
+    chunks = made.shape[0]
+    gets = [pltpu.make_async_copy(made.at[c], held.at[c], get_sem.at[c]) for c in range(chunks)]
+    for get in gets:
+        get.start()
+    puts = []
+    for c in range(chunks):
+        b, t = divmod(c, 2)
+        gets[c].wait()
+        puts.append(pltpu.make_async_copy(held.at[c], out.at[0, :, b, t], put_sem.at[c]))
+        puts[-1].start()
+    for put in puts:
+        put.wait()
+
+
 def local(n_mom, n_en, green, pair_index, pair_weight, offset, occupation, vertex, atoms):
     _, e_local, blocks, _, norb, _ = green.shape
     modes = vertex.shape[0]
@@ -228,9 +243,9 @@
     small = (pair_index, pair_weight, offset, occupation, atoms)
     dma = pltpu.SemaphoreType.DMA
     flops = 2 * e_local * chunks * modes * norb * norb * 4 * norb
-    return pl.pallas_call(
+    made = pl.pallas_call(
         functools.partial(kernel, n_mom, n_en),
-        out_shape=jax.ShapeDtypeStruct(green.shape, bf16),
+        out_shape=jax.ShapeDtypeStruct((chunks, e_local) + tile, bf16),
         in_specs=[hbm] * 7,
         out_specs=hbm,
         scratch_shapes=[pltpu.SMEM(x.shape, x.dtype) for x in small]
@@ -256,6 +271,18 @@
             flops=flops, bytes_accessed=4 * green.size, transcendentals=0
         ),
     )(green, vertex, pair_index, pair_weight, offset, occupation, atoms)
+    return pl.pallas_call(
+        deliver,
+        out_shape=jax.ShapeDtypeStruct(green.shape, bf16),
+        in_specs=[hbm],
+        out_specs=hbm,
+        scratch_shapes=[
+            pltpu.VMEM((chunks, e_local) + tile, bf16),
+            dma((chunks,)),
+            dma((chunks,)),
+        ],
+        compiler_params=pltpu.CompilerParams(vmem_limit_bytes=60 * 2**20),
+    )(made)
 
 
 def solution(mesh):

time: 20.3 us -> 20.3 us (level)
  local copies, waits for them, and re-layouts: 1.88 us -> 0 us
  Pallas kernels: 18.3 us -> 20.1 us
    unnamed x1 -> x0, local copies, waits for them, and re-layouts: 1.88 us -> none
    pallas_call x0 -> x1, Pallas kernels: none -> 1.82 us  [local(): pl.pallas_call(deliver, out_shape=jax.ShapeDtypeStruct(green.shape, bf16)...]
where the time goes in v3:
time: 20.3 us; the launch traced here: 20.1 us
  Pallas kernels  20.1 us (99%)
    pallas_call x1, Pallas kernels, local(): pl.pallas_call(functools.partial(kernel, n_mom, n_en), out_shape=jax.Shap...  18.3 us
    pallas_call x1, Pallas kernels, local(): pl.pallas_call(deliver, out_shape=jax.ShapeDtypeStruct(green.shape, bf16)...  1.82 us

profile of v3, /device:TPU:9, one launch (start us, length us, event | category | flops | bytes accessed | tf_op | source)
XLA Modules:
  0.0 20.1 jit_solution(4248220809184295788)
XLA Ops:
  0.0 18.3 %shard_map.73.made = bf16[4,8,64,128]{3,2,1,0:T(8,128)(2,1)} custom-call(bf16[1,8,2,2,64,128]{5,4,3,2,1,0:T(8,128)(2,1)} %green.1, bf16[4,8,64,64]{3,2,1,0:T(8,128)(2,1)} %vertex.1, s32[2,4]{1,0:T(2,128)} %pair_index_in.1, f32[2,4]{1,0:T(2,128)} %pair_weight_in.1, s32[4]{0:T(128)} %offset_in.1, f32[4]{0:T(128)} %occupation_in.1, s32[2,2]{1,0:T(2,128)} %atoms_in.1), custom_call_target="tpu_custom_call" | custom-call | flops 268435456 | bytes 1048576 | tf_op jit(solution)/shard_map/pallas_call | solution.py:246
  18.3 1.8 %shard_map.74 = bf16[1,8,2,2,64,128]{5,4,3,2,1,0:T(8,128)(2,1)} custom-call(bf16[4,8,64,128]{3,2,1,0:T(8,128)(2,1)} %shard_map.73.made), custom_call_target="tpu_custom_call" | custom-call | tf_op jit(solution)/shard_map/pallas_call | solution.py:274
